TPU v7x, 128 devices: a whole 4x4x4 slice. The times are simulated.
128 devices in a mesh: dp: 16 (over y, z), graph: 8 (over x, core).
Axes of the slice: x: 4, y: 4, z: 4, core: 2. Of those that a mesh axis runs over, the one named last changes fastest.
Arguments:
- nodes: bfloat16 [16, 512, 1024], P('dp', 'graph'), may hold values from -6 to 6
- node_grad: bfloat16 [16, 512, 1024], P('dp', 'graph'), may hold values from -6 to 6
- edges: bfloat16 [16, 8192, 512], P('dp', 'graph'), may hold values from -6 to 6
- source: int32 [16, 8192], P('dp', 'graph'), may hold values from 0 to 511
- target: int32 [16, 8192], P('dp', 'graph'), may hold values from 0 to 511
- trip_in: int32 [16, 16384], P('dp', 'graph'), may hold values from 0 to 8191
- trip_out: int32 [16, 16384], P('dp', 'graph'), may hold values from 0 to 1023
- basis: bfloat16 [16, 16384, 64], P('dp', 'graph'), may hold values from -6 to 6
- trip_count: int32 [16, 8], P('dp', 'graph'), may hold values from 1 to 2048, 9216 in all within a row
- w_ne: bfloat16 [2048, 512], replicated, may hold values from -0.125 to 0.125
- w_down: bfloat16 [512, 64], replicated, may hold values from -0.25 to 0.25
- w_up: bfloat16 [64, 512], replicated, may hold values from -0.75 to 0.75
- w_en: bfloat16 [512, 1024], replicated, may hold values from -0.25 to 0.25
Outputs:
- new_nodes: bfloat16 [16, 512, 1024], P('dp', 'graph')
- edge_grad: bfloat16 [16, 8192, 512], P('dp', 'graph')
- grad_ne: float32 [2048, 512], replicated
- grad_down: float32 [512, 64], replicated
- grad_up: float32 [64, 512], replicated
- grad_en: float32 [512, 1024], replicated
Inputs may be any that keep to these rules, and one draw needn't show every extreme that they name: `trip_count`: in each batch some device has exactly 2048 live triplet slots; live slots come first on a device.
All inputs are finite; a program needn't handle non-finite values.
Results may differ from a plain program's by a relative error of at most 0.019.
Values may be sent and summed in bfloat16 or wider, within the bound.
No kernel may reach another device: no remote copies, remote signals or barrier semaphores. Data moves between devices by JAX's collectives and lax.ppermute only.
A program may use at most 128 MiB of HBM per device.

v0:
```python
import jax
import jax.numpy as jnp
from jax import lax
from jax.sharding import PartitionSpec as P


def silu_grad(value):
    sig = jax.nn.sigmoid(value)
    return sig * (1.0 + value * (1.0 - sig))


def one_hot(index, start, width):
    slots = jnp.arange(width, dtype=jnp.int32)
    return ((index - start)[:, None] == slots[None, :]).astype(jnp.bfloat16)


def pick_rows(table, index, start):
    return jnp.dot(one_hot(index, start, table.shape[0]), table, preferred_element_type=jnp.float32)


def pick_exact(table, index):
    upper = table.astype(jnp.bfloat16)
    lower = (table - upper.astype(jnp.float32)).astype(jnp.bfloat16)
    hot = one_hot(index, 0, table.shape[0])
    return jnp.dot(hot, upper, preferred_element_type=jnp.float32) + jnp.dot(
        hot, lower, preferred_element_type=jnp.float32
    )


def collect_into(values, index, start, width):
    hot = one_hot(index, start, width)
    dims = (((0,), (0,)), ((), ()))
    upper = values.astype(jnp.bfloat16)
    lower = (values - upper.astype(jnp.float32)).astype(jnp.bfloat16)
    return lax.dot_general(hot, upper, dims, preferred_element_type=jnp.float32) + lax.dot_general(
        hot, lower, dims, preferred_element_type=jnp.float32
    )


def local(
    nodes,
    node_grad,
    edges,
    source,
    target,
    trip_in,
    trip_out,
    basis,
    trip_count,
    w_ne,
    w_down,
    w_up,
    w_en,
):
    all_nodes, all_grad = (
        lax.all_gather(nodes[0], "graph", axis=0, tiled=True),
        lax.all_gather(node_grad[0], "graph", axis=0, tiled=True),
    )
    node_total = all_nodes.shape[0]
    edge_local = edges.shape[1]
    src_rows = source[0]
    tgt_rows = target[0]
    in_rows = trip_in[0]
    out_rows = trip_out[0]
    basis_local = basis[0].astype(jnp.float32)
    live = (jnp.arange(in_rows.shape[0], dtype=jnp.int32) < trip_count[0, 0]).astype(jnp.float32)[
        :, None
    ]
    src_hot = one_hot(src_rows, 0, node_total)
    tgt_hot = one_hot(tgt_rows, 0, node_total)
    pair = jnp.concatenate(
        [
            jnp.dot(src_hot, all_nodes, preferred_element_type=jnp.float32),
            jnp.dot(tgt_hot, all_nodes, preferred_element_type=jnp.float32),
        ],
        axis=1,
    ).astype(jnp.bfloat16)
    pre = jnp.dot(pair, w_ne, preferred_element_type=jnp.float32)
    inner = (edges[0].astype(jnp.float32) + jax.nn.silu(pre)).astype(jnp.bfloat16)
    down = jnp.dot(inner, w_down, preferred_element_type=jnp.float32).astype(jnp.bfloat16)
    picked = pick_rows(lax.all_gather(down, "graph", axis=0, tiled=True), in_rows, jnp.int32(0))
    term = picked * basis_local * live
    summed = collect_into(term, out_rows, 0, edge_local).astype(jnp.bfloat16)
    zed = jnp.dot(summed, w_up, preferred_element_type=jnp.float32)
    outer = (inner.astype(jnp.float32) + jax.nn.silu(zed)).astype(jnp.bfloat16)
    dims = (((0,), (0,)), ((), ()))
    message = jnp.dot(outer, w_en, preferred_element_type=jnp.float32)
    upper = message.astype(jnp.bfloat16)
    lower = (message - upper.astype(jnp.float32)).astype(jnp.bfloat16)
    spread = lax.dot_general(
        tgt_hot, upper, dims, preferred_element_type=jnp.float32
    ) + lax.dot_general(tgt_hot, lower, dims, preferred_element_type=jnp.float32)
    update = lax.psum_scatter(
        spread.astype(jnp.bfloat16), "graph", scatter_dimension=0, tiled=True
    ).astype(jnp.float32)
    new_nodes = (nodes[0].astype(jnp.float32) + update).astype(jnp.bfloat16)
    back = jnp.dot(tgt_hot, all_grad, preferred_element_type=jnp.float32).astype(jnp.bfloat16)
    d_outer = jnp.dot(back, w_en.T, preferred_element_type=jnp.float32)
    g_en = jnp.dot(outer.T, back, preferred_element_type=jnp.float32)
    d_zed = (d_outer * silu_grad(zed)).astype(jnp.bfloat16)
    g_up = jnp.dot(summed.T, d_zed, preferred_element_type=jnp.float32)
    d_sum = jnp.dot(d_zed, w_up.T, preferred_element_type=jnp.float32)
    d_term = pick_exact(d_sum, out_rows) * basis_local * live
    d_down = lax.psum_scatter(
        collect_into(d_term, in_rows, jnp.int32(0), edge_local * lax.axis_size("graph")).astype(
            jnp.bfloat16
        ),
        "graph",
        scatter_dimension=0,
        tiled=True,
    )
    d_inner = d_outer + jnp.dot(d_down, w_down.T, preferred_element_type=jnp.float32)
    g_down = jnp.dot(inner.T, d_down, preferred_element_type=jnp.float32)
    d_pre = (d_inner * silu_grad(pre)).astype(jnp.bfloat16)
    g_ne = jnp.dot(pair.T, d_pre, preferred_element_type=jnp.float32)
    g_ne, g_down, g_up, g_en = lax.psum((g_ne, g_down, g_up, g_en), ("dp", "graph"))
    return (new_nodes[None], d_inner.astype(jnp.bfloat16)[None], g_ne, g_down, g_up, g_en)


def solution(mesh):
    in_specs = (
        P("dp", "graph", None),
        P("dp", "graph", None),
        P("dp", "graph", None),
        P("dp", "graph"),
        P("dp", "graph"),
        P("dp", "graph"),
        P("dp", "graph"),
        P("dp", "graph", None),
        P("dp", "graph"),
        P(),
        P(),
        P(),
        P(),
    )
    out_specs = (P("dp", "graph", None), P("dp", "graph", None), P(), P(), P(), P())
    return jax.shard_map(local, mesh=mesh, in_specs=in_specs, out_specs=out_specs, check_vma=False)
```

profile of v0, /device:TPU:1, one launch (start us, length us, event | category | flops | bytes accessed | tf_op | source)
XLA Modules:
  0.0 390.3 jit_solution(2737381019390353349)
XLA Ops:
  8.7 28.0 %all-gather.8.cloned.1.call-done = bf16[1,512,1024]{2,1,0:T(8,128)(2,1)} async-done(((bf16[1,64,1024]{2,1,0:T(8,128)(2,1)}), bf16[1,512,1024]{2,1,0:T(8,128)(2,1)}) %all-gather.8.cloned.1.call-update) | async-done | bytes 1048592 | tf_op jit(solution)/shard_map/all_gather | solution.py:56
  36.7 2.8 fusion.30
  41.5 3.9 fusion.24
  47.3 14.4 %all-gather.10.cloned.1.call-done = bf16[1,512,1024]{2,1,0:T(8,128)(2,1)} async-done(((bf16[1,64,1024]{2,1,0:T(8,128)(2,1)}), bf16[1,512,1024]{2,1,0:T(8,128)(2,1)}) %all-gather.10.cloned.1.call-update) | async-done | bytes 1048592 | tf_op jit(solution)/shard_map/all_gather | solution.py:57
  61.7 3.8 fusion.31
  65.5 23.5 %all-gather.6.cloned.1.call-done = bf16[8192,64]{1,0:T(8,128)(2,1)} async-done(((bf16[1024,64]{1,0:T(8,128)(2,1)}), bf16[8192,64]{1,0:T(8,128)(2,1)}) %all-gather.6.cloned.1.call-update) | async-done | bytes 1048592 | tf_op jit(solution)/shard_map/all_gather | solution.py:81
  89.0 16.5 %fusion.22 = f32[2048,64]{0,1:T(8,128)S(1)} fusion(bf16[8192,64]{1,0:T(8,128)(2,1)} %all-gather.6.cloned.1.call-done, s32[2048]{0:T(1024)S(1)} %bitcast.52, bf16[1,2048,64]{1,2,0:T(8,128)(2,1)} %param.20, f32[2048]{0:T(1024)S(1)} %fusion.53), kind=kOutput, calls=%fused_computation.26 | convolution fusion | flops 2164654080 | bytes 1851392 | tf_op jit(solution)/shard_map/dot_general | solution.py:18
  110.2 3.6 multiply_convert_fusion.1
  114.2 1.8 fusion.8
  116.0 1.9 fusion.20
  117.9 14.1 %fusion = f32[8192,64]{0,1:T(8,128)S(1)} fusion(s32[2048]{0:T(1024)S(1)} %bitcast.53, f32[2048,64]{0,1:T(8,128)S(1)} %fusion.20), kind=kOutput, calls=%fused_computation.1 | convolution fusion | flops 2164785152 | bytes 2629632 | tf_op jit(solution)/shard_map/dot_general | solution.py:35
  132.0 14.5 %fusion.7 = bf16[8192,64]{0,1:T(8,128)(2,1)} fusion(f32[8192,64]{0,1:T(8,128)S(1)} %fusion, s32[2048]{0:T(1024)S(1)} %bitcast.54, f32[2048,64]{0,1:T(8,128)S(1)} %fusion.20), kind=kOutput, calls=%fused_computation.8 | convolution fusion | flops 2165440512 | bytes 3678208 | tf_op jit(solution)/shard_map/dot_general | solution.py:35
  146.6 2.8 fusion.58
  150.8 2.4 add_convert_fusion
  153.5 2.2 fusion.60
  155.7 4.6 %fusion.61 = f32[512,1024]{1,0:T(8,128)} fusion(bf16[1024,512]{1,0:T(8,128)(2,1)} %get-tuple-element.11, bf16[1024,1024]{1,0:T(8,128)(2,1)} %fusion.31), kind=kOutput, calls=%fused_computation.82 | convolution fusion | flops 1073741824 | bytes 5242880 | tf_op jit(solution)/shard_map/dot_general | solution.py:99
  160.3 15.4 %reduce-scatter.5.cloned.1.call-done = bf16[1024,64]{0,1:T(8,128)(2,1)} async-done(((bf16[8192,64]{0,1:T(8,128)(2,1)}), bf16[1024,64]{0,1:T(8,128)(2,1)}) %reduce-scatter.5.cloned.1.call-update) | async-done | bytes 131088 | tf_op jit(solution)/shard_map/reduce_scatter | solution.py:104
  175.7 1.9 fusion.62
  177.6 2.3 convolution_add_fusion
  181.2 6.2 %fusion.16 = f32[2048,512]{1,0:T(8,128)} fusion(bf16[1024,1024]{0,1:T(8,128)(2,1)S(1)} %copy-done.19, bf16[1024,1024]{0,1:T(8,128)(2,1)S(1)} %copy-done.21, f32[1024,512]{1,0:T(8,128)S(1)} %convolution_add_fusion, f32[1024,512]{1,0:T(8,128)} %get-tuple-element.13), kind=kOutput, calls=%fused_computation.20 | convolution fusion | flops 2160590848 | bytes 12582912 | tf_op jit(solution)/shard_map/dot_general | solution.py:115
  187.4 21.3 %reduce-scatter.3.cloned.1.call-done = bf16[64,1024]{1,0:T(8,128)(2,1)} async-done(((bf16[512,1024]{1,0:T(8,128)(2,1)}), bf16[64,1024]{1,0:T(8,128)(2,1)}) %reduce-scatter.3.cloned.1.call-update) | async-done | bytes 131088 | tf_op jit(solution)/shard_map/reduce_scatter | solution.py:93
  210.3 2.7 convert_bitcast_fusion
  213.0 163.1 %all-reduce.3.cloned.1.call-done = (f32[2048,512]{1,0:T(8,128)}, f32[512,64]{0,1:T(8,128)}, f32[64,512]{1,0:T(8,128)}, f32[512,1024]{1,0:T(8,128)}) async-done(((f32[2048,512]{1,0:T(8,128)}, f32[512,64]{0,1:T(8,128)}, f32[64,512]{1,0:T(8,128)}, f32[512,1024]{1,0:T(8,128)}), (f32[2048,512]{1,0:T(8,128)}, f32[512,64]{0,1:T(8,128)}, f32[64,512]{1,0:T(8,128)}, ...) | async-done | bytes 6553616 | tf_op jit(solution)/shard_map/psum | solution.py:116
  376.0 4.8 %copy.24 = f32[2048,512]{1,0:T(8,128)} copy(f32[2048,512]{1,0:T(8,128)} %get-tuple-element.17) | data formatting | bytes 8388608
  (68 shorter events, 17.2 us)
Async XLA Ops:
  7.2 33.9 %copy-start = (bf16[2048,512]{1,0:T(8,128)(2,1)S(1)}, bf16[2048,512]{1,0:T(8,128)(2,1)}, u32[]{:S(2)}) copy-start(bf16[2048,512]{1,0:T(8,128)(2,1)} %param.22) | copy-start | bytes 6291460
  7.2 29.5 %all-gather.8.cloned.1.call-start = ((), (), s32[]{:S(2)}) async-start(), calls=%async_computation.5 | async-start | bytes 1179648 | tf_op jit(solution)/shard_map/all_gather | solution.py:56
  7.9 53.8 %all-gather.10.cloned.1.call-start = ((), (), s32[]{:S(2)}) async-start(), calls=%async_computation.6 | async-start | bytes 1179648 | tf_op jit(solution)/shard_map/all_gather | solution.py:57
  8.7 80.3 %all-gather.6.cloned.1.call-start = ((), (), s32[]{:S(2)}) async-start(), calls=%async_computation.2 | async-start | bytes 2359296 | tf_op jit(solution)/shard_map/all_gather | solution.py:81
  36.7 2.8 copy-start.12
  36.7 2.8 copy-start.16
  39.6 2.0 copy-start.10
  41.5 3.9 %copy-start.20 = (bf16[1024,1024]{0,1:T(8,128)(2,1)}, bf16[1024,1024]{0,1:T(8,128)(2,1)S(1)}, u32[]{:S(2)}) copy-start(bf16[1024,1024]{0,1:T(8,128)(2,1)S(1)} %fusion.29) | copy-start | bytes 6291460
  41.5 3.9 %copy-start.6 = (bf16[512,64]{0,1:T(8,128)(2,1)S(1)}, bf16[512,64]{0,1:T(8,128)(2,1)}, u32[]{:S(2)}) copy-start(bf16[512,64]{0,1:T(8,128)(2,1)} %param.23) | copy-start | bytes 196612
  41.5 20.1 %copy-start.17 = (s32[1,1024]{1,0:T(1,128)S(1)}, s32[1,1024]{1,0:T(1,128)}, u32[]{:S(2)}) copy-start(s32[1,1024]{1,0:T(1,128)} %param.17) | copy-start | bytes 12292
  46.6 129.1 %reduce-scatter.5.cloned.1.call-start = ((), (), s32[]{:S(2)}) async-start(), calls=%async_computation.4 | async-start | bytes 1179648 | tf_op jit(solution)/shard_map/reduce_scatter | solution.py:104
  47.3 41.7 %copy-start.15 = (s32[1,2048]{1,0:T(1,128)S(1)}, s32[1,2048]{1,0:T(1,128)}, u32[]{:S(2)}) copy-start(s32[1,2048]{1,0:T(1,128)} %param.18) | copy-start | bytes 24580
  89.0 16.5 %copy-start.14 = (s32[1,2048]{1,0:T(1,128)S(1)}, s32[1,2048]{1,0:T(1,128)}, u32[]{:S(2)}) copy-start(s32[1,2048]{1,0:T(1,128)} %param.19) | copy-start | bytes 24580
  107.0 2.1 copy-start.11
  113.8 2.3 copy-start.2
  114.2 1.8 copy-start.13
  146.6 62.1 %reduce-scatter.3.cloned.1.call-start = ((), (), s32[]{:S(2)}) async-start(), calls=%async_computation.3 | async-start | bytes 1179648 | tf_op jit(solution)/shard_map/reduce_scatter | solution.py:93
  153.2 222.8 %all-reduce.3.cloned.1.call-start = ((), (), s32[]{:S(2)}) async-start(), calls=%async_computation.7 | async-start | bytes 13107200 | tf_op jit(solution)/shard_map/psum | solution.py:116
  177.6 3.7 copy-start.19
  177.6 3.7 copy-start.21
  187.4 21.3 %copy-start.5 = (bf16[1,64,1024]{2,1,0:T(8,128)(2,1)S(1)}, bf16[1,64,1024]{2,1,0:T(8,128)(2,1)}, u32[]{:S(2)}) copy-start(bf16[1,64,1024]{2,1,0:T(8,128)(2,1)} %param.13) | copy-start | bytes 393220
  376.0 4.8 %copy-start.9 = (f32[512,64]{0,1:T(8,128)S(1)}, f32[512,64]{0,1:T(8,128)}, u32[]{:S(2)}) copy-start(f32[512,64]{0,1:T(8,128)} %get-tuple-element.18) | copy-start | bytes 393220
  376.0 5.5 %copy-start.8 = (f32[64,512]{1,0:T(8,128)S(1)}, f32[64,512]{1,0:T(8,128)}, u32[]{:S(2)}) copy-start(f32[64,512]{1,0:T(8,128)} %get-tuple-element.19) | copy-start | bytes 393220
  376.0 6.1 %copy-start.4 = (f32[512,1024]{1,0:T(8,128)S(1)}, f32[512,1024]{1,0:T(8,128)}, u32[]{:S(2)}) copy-start(f32[512,1024]{1,0:T(8,128)} %get-tuple-element.20) | copy-start | bytes 6291460
  (4 other events, 6.1 us)
Sparse Core Ops, SparseCore 0:
  9.7 26.9 all-gather.7
  38.4 23.1 all-gather.9
  64.0 24.9 all-gather.5
  146.7 28.9 reduce-scatter.4
  177.9 30.7 reduce-scatter.2
  214.7 161.2 all-reduce.2
where the time goes:
time: 391 us; the launch traced here: 390 us
  waiting for transfers between devices  267 us (68%)
  matrix products  93 us (24%)
  between operations  15 us (4%)
  local copies, waits for them, and re-layouts  10.5 us (3%)
  other arithmetic  4.29 us (1%)
    psum x1, waiting for transfers between devices, local(): lax.psum((g_ne, g_down, g_up, g_en), ('dp', 'graph'))  163 us
    all_gather x1, waiting for transfers between devices, local(): lax.all_gather(nodes[0], 'graph', axis=0, tiled=True)  28 us
    all_gather x1, waiting for transfers between devices, local(): lax.all_gather(down, 'graph', axis=0, tiled=True)  23.5 us
    reduce_scatter x1, waiting for transfers between devices, local(): lax.psum_scatter(spread.astype(jnp.bfloat16), 'graph', scatter_dimension=...  21.3 us
    dot_general x1, matrix products, pick_rows(): jnp.dot(one_hot(index, start, table.shape[0]), table, preferred_element_t...  16.5 us
    dot_general x2, matrix products, collect_into(): lax.dot_general(hot, upper, dims, preferred_element_type=jnp.float32)  16.1 us
    dot_general x2, matrix products, collect_into(): lax.dot_general(hot, lower, dims, preferred_element_type=jnp.float32)  15.6 us
    reduce_scatter x1, waiting for transfers between devices, local(): lax.psum_scatter(collect_into(d_term, in_rows, jnp.int32(0), edge_local *...  15.4 us
  transfers between devices with their start and end apart: 6, of which 6 were waited for; matrix products, arithmetic and copies ran while one was open for 11% of the time, Pallas kernels for 0%

commit v1 on v0

v1 whole, which is shorter than its diff:
```python
import jax
import jax.numpy as jnp
from jax import lax
from jax.experimental import pallas as pl
from jax.experimental.pallas import tpu as pltpu
from jax.sharding import PartitionSpec as P

BF = jnp.bfloat16
F32 = jnp.float32
NT = (((1,), (1,)), ((), ()))


def dot(a, b):
    return jnp.dot(a, b, preferred_element_type=F32)


def dot_nt(a, b):
    return lax.dot_general(a, b, NT, preferred_element_type=F32)


def call(body, outs, args, scalars=0, scratch=(), flops=0, vmem=40):
    moved = sum(a.size * a.dtype.itemsize for a in args) + sum(
        o.size * o.dtype.itemsize for o in outs
    )
    specs = [
        pl.BlockSpec(memory_space=pltpu.SMEM if i < scalars else pltpu.VMEM)
        for i in range(len(args))
    ]
    return pl.pallas_call(
        body,
        out_shape=list(outs),
        in_specs=specs,
        out_specs=[pl.BlockSpec(memory_space=pltpu.VMEM)] * len(outs),
        scratch_shapes=list(scratch),
        compiler_params=pltpu.CompilerParams(vmem_limit_bytes=vmem << 20),
        cost_estimate=pl.CostEstimate(flops=flops, bytes_accessed=moved, transcendentals=0),
    )(*args)


def sds(shape, dtype=BF):
    return jax.ShapeDtypeStruct(shape, dtype)


def at(i, size):
    return pl.ds(pl.multiple_of(i * size, size), size)


def hot(mask):
    return jnp.where(mask, 1.0, 0.0).astype(BF)


def prep_body(cnt, src_c, tgt_c, src_r, tgt_r, in_c, in_r, out_c, out_r, s, st, il, ilt, ol, olt):
    lane = lax.broadcasted_iota(jnp.int32, (256, 512), 1)
    for i in range(4):
        ch = slice(256 * i, 256 * i + 256)
        s[ch, 0:512] = hot(src_c[ch, :] == lane)
        s[ch, 512:1024] = hot(tgt_c[ch, :] == lane)
    row = lax.broadcasted_iota(jnp.int32, (128, 1024), 0)
    for i in range(4):
        ch = slice(128 * i, 128 * i + 128)
        st[ch, :] = hot(src_r[...] == row + 128 * i)
        st[512 + 128 * i : 640 + 128 * i, :] = hot(tgt_r[...] == row + 128 * i)
    live = cnt[0, 0]
    for i in range(8):
        ch = slice(256 * i, 256 * i + 256)
        pos = lax.broadcasted_iota(jnp.int32, (256, 1), 0) + 256 * i
        il[ch, :] = hot(jnp.where(pos < live, in_c[ch, :] & 511, -1) == lane)
        ol[ch, :] = hot((out_c[ch, :] & 511) == lane)
    pos = lax.broadcasted_iota(jnp.int32, (1, 2048), 1)
    in_lo = jnp.where(pos < live, in_r[...] & 511, -1)
    out_lo = out_r[...] & 511
    row = lax.broadcasted_iota(jnp.int32, (64, 2048), 0)
    for i in range(8):
        ch = slice(64 * i, 64 * i + 64)
        ilt[ch, :] = hot(in_lo == row + 64 * i)
        olt[ch, :] = hot(out_lo == row + 64 * i)


def k1_body(
    xc, n0, n1, n2, n3, m0, m1, m2, m3, s, edges, w_ne, wd, nodes_all, dsilu, inner, down, ab
):
    x, c = xc[0], xc[1]
    for k, (mine, other) in enumerate(((n0, m0), (n1, m1), (n2, m2), (n3, m3))):
        g = 2 * lax.rem(x + 4 - k, 4)
        nodes_all[at(g + c, 64), :] = mine[...]
        nodes_all[at(g + 1 - c, 64), :] = other[...]
    for i in range(2):
        ch = slice(256 * i, 256 * i + 256)
        part = nodes_all[ch, :]
        ab[ch, :] = dot(part, w_ne[0:1024, :]).astype(BF)
        ab[512 + 256 * i : 768 + 256 * i, :] = dot(part, w_ne[1024:2048, :]).astype(BF)
    for i in range(2):
        total = None
        for h in range(2):
            ch = slice(512 * h + 256 * i, 512 * h + 256 * i + 256)
            pre = dot(s[ch, :], ab[...])
            sig = jax.nn.sigmoid(pre)
            held = (edges[ch, :].astype(F32) + pre * sig).astype(BF)
            inner[ch, :] = held
            dsilu[ch, :] = (sig * (1.0 + pre * (1.0 - sig))).astype(BF)
            part = dot(held, wd[512 * h : 512 * h + 512, :])
            total = part if total is None else total + part
        down[256 * i : 256 * i + 256, :] = total.astype(BF)


def kq_body(all_grad, w_en, s, nodes_all, d_outer, nodes_t, q):
    for i in range(2):
        ch = slice(256 * i, 256 * i + 256)
        q[ch, :] = dot_nt(all_grad[ch, :], w_en[...]).astype(BF)
    for i in range(4):
        ch = slice(256 * i, 256 * i + 256)
        d_outer[ch, :] = dot(s[ch, 512:1024], q[...]).astype(BF)
    nodes_t[...] = nodes_all[...].T


def halves(value, odd, upper):
    kept = jnp.where(upper == odd, value, 0.0)
    return kept + pltpu.roll(kept, 64, 1)


def k2_body(
    xc, d0, d1, d2, d3, e0, e1, e2, e3, il, ilt, ol, olt, in_c, out_c, basis, inner, d_outer, wu,
    keep, send, outer, summed, dzed, table, gath, spread,
):
    x, c = xc[0], xc[1]
    for k, (mine, other) in enumerate(((d0, e0), (d1, e1), (d2, e2), (d3, e3))):
        g = 2 * lax.rem(x + 4 - k, 4)
        table[:, at(g + c, 128)] = mine[...]
        table[:, at(g + 1 - c, 128)] = other[...]
    upper = lax.broadcasted_iota(jnp.int32, (256, 128), 1) >= 64
    for i in range(8):
        ch = slice(256 * i, 256 * i + 256)
        got = dot(il[ch, :], table[...])
        hi = in_c[ch, :] >> 9
        acc = jnp.zeros((256, 128), F32)
        for g in range(8):
            acc = jnp.where((hi >> 1) == g, got[:, 128 * g : 128 * g + 128], acc)
        term = halves(acc, (hi & 1) == 1, upper) * basis[ch, :].astype(F32)
        gath[ch, :] = jnp.where(upper == ((out_c[ch, :] >> 9) == 1), term, 0.0).astype(BF)
    held = dot(olt[...], gath[...]).astype(BF)
    summed[...] = held
    d_sum = jnp.zeros((512, 128), F32)
    for h in range(2):
        ch = slice(512 * h, 512 * h + 512)
        w = wu[128 * h : 128 * h + 128, :]
        zed = dot(held, w)
        sig = jax.nn.sigmoid(zed)
        outer[ch, :] = (inner[ch, :].astype(F32) + zed * sig).astype(BF)
        dz = (d_outer[ch, :].astype(F32) * (sig * (1.0 + zed * (1.0 - sig)))).astype(BF)
        dzed[ch, :] = dz
        d_sum += dot_nt(dz, w)
    d_sum = d_sum.astype(BF)
    for i in range(8):
        ch = slice(256 * i, 256 * i + 256)
        got = dot(ol[ch, :], d_sum)
        term = halves(got, (out_c[ch, :] >> 9) == 1, upper) * basis[ch, :].astype(F32)
        hi = in_c[ch, :] >> 9
        term = jnp.where(upper == ((hi & 1) == 1), term, 0.0)
        for g in range(8):
            spread[ch, 128 * g : 128 * g + 128] = jnp.where((hi >> 1) == g, term, 0.0).astype(BF)
    for i in range(4):
        ch = slice(128 * i, 128 * i + 128)
        part = dot(ilt[...], spread[:, 256 * i : 256 * i + 256])
        low, high = part[:, 0:128], part[:, 128:256]
        keep[:, ch] = jnp.where(c == 0, low, high)
        send[:, ch] = jnp.where(c == 0, high, low).astype(BF)


def ko_body(outer, st, summed, dzed, o, ot, gup):
    for i in range(2):
        ch = slice(256 * i, 256 * i + 256)
        part = dot(st[512 + 256 * i : 768 + 256 * i, :], outer[...])
        o[ch, :] = part.astype(BF)
        ot[:, ch] = part.T.astype(BF)
    summed_t = summed[...].T
    gup[...] = dot(summed_t[0:64, :], dzed[0:512, :]) + dot(summed_t[64:128, :], dzed[512:1024, :])


def ka_body(xc, keep, recv, own, s1, s2, s3):
    x = xc[0]
    for k, ref in enumerate((own, s1, s2, s3)):
        ch = at(lax.rem(x + k, 4), 128)
        ref[...] = (keep[:, ch] + recv[:, ch].astype(F32)).astype(BF)


def total4(a, b, c, d):
    return (a.astype(F32) + c.astype(F32)) + (b.astype(F32) + d.astype(F32))


def k3_body(
    xc, own, r1, r2, r3, d_outer, dsilu, inner, st, wdt, ot, gup, edge_grad, keep, send, d_pre
):
    c = xc[1]
    dd = total4(own[...], r1[...], r2[...], r3[...]).astype(BF)
    for h in range(2):
        for i in range(2):
            rows = slice(256 * i, 256 * i + 256)
            ch = slice(512 * h + 256 * i, 512 * h + 256 * i + 256)
            d_inner = d_outer[ch, :].astype(F32) + dot(dd[rows, :], wdt[128 * h : 128 * h + 128, :])
            edge_grad[ch, :] = d_inner.astype(BF)
            d_pre[ch, :] = (d_inner * dsilu[ch, :].astype(F32)).astype(BF)
    for i in range(2):
        rows = slice(256 * i, 256 * i + 256)
        send[rows, :] = dot(st[at(2 * (1 - c) + i, 256), :], d_pre[...]).astype(BF)
        keep[rows, :] = dot(st[at(2 * c + i, 256), :], d_pre[...])
    ddt = dd.T
    gdown = dot(ddt[0:64, :], inner[0:512, :]) + dot(ddt[64:128, :], inner[512:1024, :])
    keep[512:576, :] = jnp.where(c == 0, gup[...], gdown)
    send[512:576, :] = jnp.where(c == 0, gdown, gup[...]).astype(BF)
    for i in range(4):
        rows = slice(576 + 64 * i, 640 + 64 * i)
        keep[rows, :] = ot[at(2 * i + c, 64), :].astype(F32)
        send[rows, :] = ot[at(2 * i + 1 - c, 64), :]


def kb_body(xc, keep, recv, own, s1, s2, s3):
    x = xc[0]
    for k, ref in enumerate((own, s1, s2, s3)):
        b = lax.rem(x + k, 4)
        ch = at(b, 128)
        ref[0:576, :] = (keep[0:576, ch] + recv[0:576, ch].astype(F32)).astype(BF)
        rows = pl.ds(pl.multiple_of(576 + 64 * b, 64), 64)
        part = (keep[rows, :] + recv[rows, :].astype(F32)).astype(BF)
        for j in range(4):
            ref[576 + 64 * j : 640 + 64 * j, :] = part[:, 128 * j : 128 * j + 128]


def k4_body(yz, own, r1, r2, r3, nodes_t, all_grad, g0, s1, s2, s3, whole):
    y = yz[0]
    sums = total4(own[...], r1[...], r2[...], r3[...])
    whole[0:1024, :] = dot(nodes_t[...], sums[0:512, :].astype(BF)).astype(BF)
    ot = sums[576:832, :].astype(BF)
    ot = jnp.concatenate([ot[64 * j : 64 * j + 64, :] for j in range(4)], axis=1)
    gen = dot(ot, all_grad[...]).astype(BF)
    for j in range(8):
        whole[1024 + 64 * j : 1088 + 64 * j, :] = gen[:, 128 * j : 128 * j + 128]
    whole[1536:1600, :] = sums[512:576, :].astype(BF)
    for k, ref in enumerate((g0, s1, s2, s3)):
        ref[...] = whole[at(lax.rem(y + k, 4), 400), :]


def sum_body(a, b, c, d, out):
    out[...] = total4(a[...], b[...], c[...], d[...]).astype(BF)


def place_body(yz, own, r1, r2, r3, out):
    y = yz[0]
    for k, ref in enumerate((own, r1, r2, r3)):
        out[at(lax.rem(y + 4 - k, 4), 400), :] = ref[...]


def end_body(xc, p0, p1, p2, p3, q0, q1, q2, q3, gne, gdt, gup, gen):
    x, c = xc[0], xc[1]
    for k, (mine, other) in enumerate(((p0, q0), (p1, q1), (p2, q2), (p3, q3))):
        b = lax.rem(x + 4 - k, 4)
        ch = at(b, 128)
        for ref, core in ((mine, c), (other, 1 - c)):
            gne[at(core, 1024), ch] = ref[0:1024, :].astype(F32)
            rows = at(2 * b + core, 64)
            for j in range(8):
                gen[rows, 128 * j : 128 * j + 128] = ref[1024 + 64 * j : 1088 + 64 * j, :].astype(
                    F32
                )
        low = jnp.where(c == 0, mine[1536:1600, :].astype(F32), other[1536:1600, :].astype(F32))
        high = jnp.where(c == 0, other[1536:1600, :].astype(F32), mine[1536:1600, :].astype(F32))
        gup[:, ch] = low
        gdt[:, ch] = high


def over_x(value, k):
    perm = [(2 * x + c, 2 * ((x + k) % 4) + c) for x in range(4) for c in range(2)]
    return lax.ppermute(value, "graph", perm)


def over_core(value):
    return lax.ppermute(value, "graph", [(i, i ^ 1) for i in range(8)])


def over_y(value, k):
    perm = [(4 * y + z, 4 * ((y + k) % 4) + z) for y in range(4) for z in range(4)]
    return lax.ppermute(value, "dp", perm)


def over_z(value, k):
    perm = [(4 * y + z, 4 * y + (z + k) % 4) for y in range(4) for z in range(4)]
    return lax.ppermute(value, "dp", perm)


def gather8(value):
    mine = [value] + [over_x(value, k) for k in (1, 2, 3)]
    return mine + [over_core(v) for v in mine]


def local(
    nodes, node_grad, edges, source, target, trip_in, trip_out, basis, trip_count,
    w_ne, w_down, w_up, w_en,
):
    g = lax.axis_index("graph")
    d = lax.axis_index("dp")
    xc = jnp.stack([g // 2, g % 2]).astype(jnp.int32)
    yz = jnp.stack([d // 4, d % 4]).astype(jnp.int32)
    node_parts = gather8(nodes[0])
    all_grad = lax.all_gather(node_grad[0], "graph", axis=0, tiled=True)

    in_c, out_c = trip_in[0][:, None], trip_out[0][:, None]
    s, st, il, ilt, ol, olt = call(
        prep_body,
        [sds((1024, 1024)), sds((1024, 1024)), sds((2048, 512)), sds((512, 2048)),
         sds((2048, 512)), sds((512, 2048))],
        [trip_count, source[0][:, None], target[0][:, None], source, target,
         in_c, trip_in, out_c, trip_out],
        scalars=1, flops=1 << 22,
    )
    none = jnp.zeros((512, 64), BF)
    wd = jnp.concatenate(
        [jnp.concatenate([w_down, none], axis=1), jnp.concatenate([none, w_down], axis=1)], axis=0
    )
    wu = jnp.concatenate([w_up, none.T, none.T, w_up], axis=0)
    wdt = jnp.concatenate([w_down.T, none.T, none.T, w_down.T], axis=0)
    basis2 = jnp.concatenate([basis[0], basis[0]], axis=1)

    nodes_all, dsilu, inner, down = call(
        k1_body,
        [sds((512, 1024)), sds((1024, 512)), sds((1024, 512)), sds((512, 128))],
        [xc, *node_parts, s, edges[0], w_ne, wd],
        scalars=1, scratch=[pltpu.VMEM((1024, 512), BF)], flops=2 << 30,
    )
    down_parts = gather8(down)
    d_outer, nodes_t = call(
        kq_body,
        [sds((1024, 512)), sds((1024, 512))],
        [all_grad, w_en, s, nodes_all],
        scratch=[pltpu.VMEM((512, 512), BF)], flops=1 << 30,
    )
    keep, send, outer, summed, dzed = call(
        k2_body,
        [sds((512, 512), F32), sds((512, 512)), sds((1024, 512)), sds((512, 128)),
         sds((1024, 512))],
        [xc, *down_parts, il, ilt, ol, olt, in_c, out_c, basis2, inner, d_outer, wu],
        scalars=1,
        scratch=[pltpu.VMEM((512, 1024), BF), pltpu.VMEM((2048, 128), BF),
                 pltpu.VMEM((2048, 1024), BF)],
        flops=4 << 30,
    )
    recv = over_core(send)
    parts = call(ka_body, [sds((512, 128))] * 4, [xc, keep, recv], scalars=1)
    dd = [parts[0]] + [over_x(parts[k], k) for k in (1, 2, 3)]
    o, ot, gup = call(
        ko_body,
        [sds((512, 512)), sds((512, 512)), sds((64, 512), F32)],
        [outer, st, summed, dzed], flops=1 << 29,
    )
    edge_grad, keep, send = call(
        k3_body,
        [sds((1024, 512)), sds((832, 512), F32), sds((832, 512))],
        [xc, *dd, d_outer, dsilu, inner, st, wdt, ot, gup],
        scalars=1, scratch=[pltpu.VMEM((1024, 512), BF)], flops=2 << 30,
    )
    recv = over_core(send)
    parts = call(kb_body, [sds((832, 128))] * 4, [xc, keep, recv], scalars=1)
    parts = [parts[0]] + [over_x(parts[k], k) for k in (1, 2, 3)]
    parts = call(
        k4_body, [sds((400, 128))] * 4, [yz, *parts, nodes_t, all_grad],
        scalars=1, scratch=[pltpu.VMEM((1600, 128), BF)], flops=1 << 28,
    )
    parts = [parts[0]] + [over_y(parts[k], k) for k in (1, 2, 3)]
    (part,) = call(sum_body, [sds((400, 128))], parts)
    (part,) = call(sum_body, [sds((400, 128))], [part] + [over_z(part, k) for k in (1, 2, 3)])
    parts = [part] + [over_y(part, k) for k in (1, 2, 3)]
    (part,) = call(place_body, [sds((1600, 128))], [yz, *parts], scalars=1)
    grad_ne, grad_down_t, grad_up, grad_en = call(
        end_body,
        [sds((2048, 512), F32), sds((64, 512), F32), sds((64, 512), F32), sds((512, 1024), F32)],
        [xc, *gather8(part)],
        scalars=1,
    )
    rows = lax.psum_scatter(o, "graph", scatter_dimension=0, tiled=True)
    new_nodes = (nodes[0].astype(F32) + dot(rows, w_en)).astype(BF)
    return (new_nodes[None], edge_grad[None], grad_ne, grad_down_t.T, grad_up, grad_en)


def solution(mesh):
    split3, split2 = P("dp", "graph", None), P("dp", "graph")
    in_specs = (split3,) * 3 + (split2,) * 4 + (split3, split2) + (P(),) * 4
    out_specs = (split3, split3, P(), P(), P(), P())
    return jax.shard_map(local, mesh=mesh, in_specs=in_specs, out_specs=out_specs, check_vma=False)
```

time: 391 us -> 179 us (0.46)
  waiting for transfers between devices: 267 us -> 44.9 us
  matrix products: 93 us -> 1.9 us
  starting transfers between devices: 0.5 us -> 56.8 us
  Pallas kernels: 0 us -> 35.3 us
  local copies, waits for them, and re-layouts: 10.5 us -> 20.6 us
    psum x1 -> x0, waiting for transfers between devices: 163 us -> none  [local(): lax.psum((g_ne, g_down, g_up, g_en), ('dp', 'graph'))]
    dot_general x23 -> x1, matrix products: 93 us -> 1.9 us  [dot(): return jnp.dot(a, b, preferred_element_type=F32)]
    all_gather x3 -> x1, waiting for transfers between devices: 65.9 us -> 0.01 us  [local(): all_grad = lax.all_gather(node_grad[0], 'graph', axis=0, tiled=True)]
    ppermute x0 -> x38, starting transfers between devices: none -> 56.7 us  [the longest x14 29 us: over_core(): return lax.ppermute(value, 'graph', [(i, i ^ 1) for i in range(8)])]
    ppermute x0 -> x38, waiting for transfers between devices: none -> 44.2 us  [the longest x15 26.2 us: over_x(): return lax.ppermute(value, 'graph', perm)]
    reduce_scatter x2 -> x1, waiting for transfers between devices: 36.7 us -> 0.01 us  [local(): rows = lax.psum_scatter(o, 'graph', scatter_dimension=0, tiled=True)]
    pallas_call x0 -> x13, Pallas kernels: none -> 35.3 us  [call(): pl.pallas_call(body, out_shape=list(outs), in_specs=specs, out_specs=[pl....]
    unnamed x48 -> x68, local copies, waits for them, and re-layouts: 10.5 us -> 18 us
  transfers between devices with their start and end apart: 6 -> 40, of which waited for: 6 -> 22; matrix products, arithmetic and copies ran while one was open for 11% -> 7% of each run, Pallas kernels for 0% -> 8%
where the time goes in v1:
time: 179 us; the launch traced here: 178 us
  starting transfers between devices  56.8 us (32%)
  waiting for transfers between devices  44.9 us (25%)
  Pallas kernels  35.3 us (20%)
  local copies, waits for them, and re-layouts  20.6 us (12%)
  between operations  15.1 us (8%)
  other arithmetic  3.49 us (2%)
  matrix products  1.9 us (1%)
    pallas_call x13, Pallas kernels, call(): pl.pallas_call(body, out_shape=list(outs), in_specs=specs, out_specs=[pl....  35.3 us
    ppermute x14, starting transfers between devices, over_core(): return lax.ppermute(value, 'graph', [(i, i ^ 1) for i in range(8)])  29 us
    ppermute x15, waiting for transfers between devices, over_x(): return lax.ppermute(value, 'graph', perm)  26.2 us
    unnamed x68, local copies, waits for them, and re-layouts  18 us
    ppermute x15, starting transfers between devices, over_x(): return lax.ppermute(value, 'graph', perm)  15.2 us
    ppermute x6, waiting for transfers between devices, over_y(): return lax.ppermute(value, 'dp', perm)  8.92 us
    ppermute x6, starting transfers between devices, over_y(): return lax.ppermute(value, 'dp', perm)  7.97 us
    ppermute x3, waiting for transfers between devices, over_z(): return lax.ppermute(value, 'dp', perm)  5.15 us
  transfers between devices with their start and end apart: 40, of which 22 were waited for; matrix products, arithmetic and copies ran while one was open for 7% of the time, Pallas kernels for 8%

profile of v1, /device:TPU:1, one launch (start us, length us, event | category | flops | bytes accessed | tf_op | source)
XLA Modules:
  0.0 178.0 jit_solution(16163478039008054736)
XLA Ops:
  8.0 3.4 %collective-permute-start.2 = (bf16[64,1024]{1,0:T(8,128)(2,1)}, bf16[64,1024]{1,0:T(8,128)(2,1)}, u32[]{:S(2)}, u32[]{:S(2)}) collective-permute-start(bf16[64,1024]{1,0:T(8,128)(2,1)} %bitcast.22), channel_id=1, source_target_pairs={{0,6},{1,7},{2,0},{3,1},{4,2},{5,3},{6,4},{7,5},{8,14},{9,15},{10,... | collective-permute-start | bytes 393224 | tf_op jit(solution)/shard_map/ppermute | solution.py:272
  14.0 2.6 %collective-permute-done.2.n3 = bf16[64,1024]{1,0:T(8,128)(2,1)} collective-permute-done((bf16[64,1024]{1,0:T(8,128)(2,1)}, bf16[64,1024]{1,0:T(8,128)(2,1)}, u32[]{:S(2)}, u32[]{:S(2)}) %collective-permute-start.2) | collective-permute-done | bytes 131104 | tf_op jit(solution)/shard_map/ppermute | solution.py:272
  18.2 2.3 %collective-permute-start.5 = (bf16[64,1024]{1,0:T(8,128)(2,1)}, bf16[64,1024]{1,0:T(8,128)(2,1)}, u32[]{:S(2)}, u32[]{:S(2)}) collective-permute-start(bf16[64,1024]{1,0:T(8,128)(2,1)} %collective-permute-done.1.n2), channel_id=1, source_target_pairs={{0,1},{1,0},{2,3},{3,2},{4,5},{5,4},{6,7},{7,6},{8,9},{9,8},{10,11... | collective-permute-start | bytes 393224 | tf_op jit(solution)/shard_map/ppermute | solution.py:276
  28.9 4.2 %shard_map.172 = (bf16[1024,1024]{1,0:T(8,128)(2,1)S(1)}, bf16[1024,1024]{1,0:T(8,128)(2,1)S(1)}, bf16[2048,512]{1,0:T(8,128)(2,1)S(1)}, bf16[512,2048]{1,0:T(8,...) custom-call(s32[1,1]{1,0:T(1,128)S(6)} %copy.31.cnt, s32[1024,1]{1,0:T(8,128)S(1)} %copy.22.src_c, ...), custom_call_target="tpu_custom_call" | custom-call | flops 4194304 | bytes 12632068 | tf_op jit(solution)/shard_map/pallas_call | solution.py:29
  38.7 5.2 %shard_map.173 = (bf16[512,1024]{1,0:T(8,128)(2,1)S(1)}, bf16[1024,512]{1,0:T(8,128)(2,1)S(1)}, bf16[1024,512]{1,0:T(8,128)(2,1)S(1)}, bf16[512,128]{1,0:T(8,128)(2,1)}) custom-call(s32[2]{0:T(128)S(1)} %pad_add_fusion.xc, bf16[64,1024]{1,0:T(8,128)(2,1)S(1)} %bitcast.26, bf16[64,1024]{1,0:T(8,128)(2,1)} %collective-permute-done.n1, ...), custom_call_target="tpu_custom_call" | custom-call | flops 2147483648 | bytes 9830408 | tf_op jit(solution)/shard_map/pallas_call | solution.py:29
  49.9 2.4 %collective-permute-done.9.d3 = bf16[512,128]{1,0:T(8,128)(2,1)} collective-permute-done((bf16[512,128]{1,0:T(8,128)(2,1)}, bf16[512,128]{1,0:T(8,128)(2,1)}, u32[]{:S(2)}, u32[]{:S(2)}) %collective-permute-start.9) | collective-permute-done | bytes 131104 | tf_op jit(solution)/shard_map/ppermute | solution.py:272
  66.8 11.8 %shard_map.175 = (f32[512,512]{1,0:T(8,128)S(1)}, bf16[512,512]{1,0:T(8,128)(2,1)S(1)}, bf16[1024,512]{1,0:T(8,128)(2,1)S(1)}, bf16[512,128]{1,0:T(8,128)(2,1)S(1)}, bf16[1024,512]{1,0:T(8,128)(2,1)S(1)}) custom-call(s32[2]{0:T(128)S(1)} %pad_add_fusion.xc, bf16[512,128]{1,0:T(8,128)(2,1)} %get-tuple-element.46.d0, ...), custom_call_target="tpu_custom_call" | custom-call | flops 4294967296 | bytes 16138248 | tf_op jit(solution)/shard_map/pallas_call | solution.py:29
  85.8 4.6 %collective-permute-done.15.r1 = bf16[512,128]{1,0:T(8,128)(2,1)S(1)} collective-permute-done((bf16[512,128]{1,0:T(8,128)(2,1)S(1)}, bf16[512,128]{1,0:T(8,128)(2,1)S(1)}, u32[]{:S(2)}, u32[]{:S(2)}) %collective-permute-start.15) | collective-permute-done | bytes 131104 | tf_op jit(solution)/shard_map/ppermute | solution.py:272
  90.7 2.5 %shard_map.178 = (bf16[1024,512]{1,0:T(8,128)(2,1)}, f32[832,512]{1,0:T(8,128)S(1)}, bf16[832,512]{1,0:T(8,128)(2,1)S(1)}) custom-call(s32[2]{0:T(128)S(1)} %pad_add_fusion.xc, bf16[512,128]{1,0:T(8,128)(2,1)S(1)} %get-tuple-element.61.own, bf16[512,128]{1,0:T(8,128)(2,1)S(1)} %collective-permute-done.15.r1, ...), custom_call_target="tpu_custom_call" | custom-call | flops 2147483648 | bytes 10289160 | tf_op jit(solution)/shard_map/pallas_call | solution.py:29
  98.0 3.2 %collective-permute-start.20 = (bf16[832,128]{1,0:T(8,128)(2,1)}, bf16[832,128]{1,0:T(8,128)(2,1)}, u32[]{:S(2)}, u32[]{:S(2)}) collective-permute-start(bf16[832,128]{1,0:T(8,128)(2,1)} %get-tuple-element.73), channel_id=1, source_target_pairs={{0,4},{1,5},{2,6},{3,7},{4,0},{5,1},{6,2},{7,3},{8,12},{9,13},{10,... | collective-permute-start | bytes 638984 | tf_op jit(solution)/shard_map/ppermute | solution.py:272
  101.4 4.6 %collective-permute-done.19.r1 = bf16[832,128]{1,0:T(8,128)(2,1)} collective-permute-done((bf16[832,128]{1,0:T(8,128)(2,1)}, bf16[832,128]{1,0:T(8,128)(2,1)}, u32[]{:S(2)}, u32[]{:S(2)}) %collective-permute-start.19) | collective-permute-done | bytes 213024 | tf_op jit(solution)/shard_map/ppermute | solution.py:272
  106.0 5.1 %collective-permute-done.20.r2 = bf16[832,128]{1,0:T(8,128)(2,1)} collective-permute-done((bf16[832,128]{1,0:T(8,128)(2,1)}, bf16[832,128]{1,0:T(8,128)(2,1)}, u32[]{:S(2)}, u32[]{:S(2)}) %collective-permute-start.20) | collective-permute-done | bytes 213024 | tf_op jit(solution)/shard_map/ppermute | solution.py:272
  114.3 2.6 %collective-permute-start.23 = (bf16[400,128]{1,0:T(8,128)(2,1)S(1)}, bf16[400,128]{1,0:T(8,128)(2,1)S(1)}, u32[]{:S(2)}, u32[]{:S(2)}) collective-permute-start(bf16[400,128]{1,0:T(8,128)(2,1)S(1)} %get-tuple-element.78), channel_id=1, source_target_pairs={{0,64},{8,72},{16,80},{24,88},{32,96},{40,104},{48,112},{56,120},{... | collective-permute-start | bytes 307208 | tf_op jit(solution)/shard_map/ppermute | solution.py:281
  118.1 2.4 %collective-permute-done.23.c = bf16[400,128]{1,0:T(8,128)(2,1)S(1)} collective-permute-done((bf16[400,128]{1,0:T(8,128)(2,1)S(1)}, bf16[400,128]{1,0:T(8,128)(2,1)S(1)}, u32[]{:S(2)}, u32[]{:S(2)}) %collective-permute-start.23) | collective-permute-done | bytes 102432 | tf_op jit(solution)/shard_map/ppermute | solution.py:281
  121.9 3.8 %collective-permute-start.27 = (bf16[400,128]{1,0:T(8,128)(2,1)S(1)}, bf16[400,128]{1,0:T(8,128)(2,1)S(1)}, u32[]{:S(2)}, u32[]{:S(2)}) collective-permute-start(bf16[400,128]{1,0:T(8,128)(2,1)S(1)} %shard_map.181.a), channel_id=1, source_target_pairs={{0,24},{8,0},{16,8},{24,16},{32,56},{40,32},{48,40},{56,48},{64,88... | collective-permute-start | bytes 307208 | tf_op jit(solution)/shard_map/ppermute | solution.py:286
  126.4 2.0 %collective-permute-done.27.d = bf16[400,128]{1,0:T(8,128)(2,1)S(1)} collective-permute-done((bf16[400,128]{1,0:T(8,128)(2,1)S(1)}, bf16[400,128]{1,0:T(8,128)(2,1)S(1)}, u32[]{:S(2)}, u32[]{:S(2)}) %collective-permute-start.27) | collective-permute-done | bytes 102432 | tf_op jit(solution)/shard_map/ppermute | solution.py:286
  128.4 2.4 %collective-permute-done.26.c = bf16[400,128]{1,0:T(8,128)(2,1)S(1)} collective-permute-done((bf16[400,128]{1,0:T(8,128)(2,1)S(1)}, bf16[400,128]{1,0:T(8,128)(2,1)S(1)}, u32[]{:S(2)}, u32[]{:S(2)}) %collective-permute-start.26) | collective-permute-done | bytes 102432 | tf_op jit(solution)/shard_map/ppermute | solution.py:286
  131.6 2.2 %collective-permute-start.30 = (bf16[400,128]{1,0:T(8,128)(2,1)S(1)}, bf16[400,128]{1,0:T(8,128)(2,1)S(1)}, u32[]{:S(2)}, u32[]{:S(2)}) collective-permute-start(bf16[400,128]{1,0:T(8,128)(2,1)S(1)} %shard_map.182.own), channel_id=1, source_target_pairs={{0,96},{8,104},{16,112},{24,120},{32,0},{40,8},{48,16},{56,24},{64... | collective-permute-start | bytes 307208 | tf_op jit(solution)/shard_map/ppermute | solution.py:281
  134.5 2.0 %collective-permute-done.30.r3 = bf16[400,128]{1,0:T(8,128)(2,1)S(1)} collective-permute-done((bf16[400,128]{1,0:T(8,128)(2,1)S(1)}, bf16[400,128]{1,0:T(8,128)(2,1)S(1)}, u32[]{:S(2)}, u32[]{:S(2)}) %collective-permute-start.30) | collective-permute-done | bytes 102432 | tf_op jit(solution)/shard_map/ppermute | solution.py:281
  136.5 2.4 %collective-permute-done.29.r2 = bf16[400,128]{1,0:T(8,128)(2,1)S(1)} collective-permute-done((bf16[400,128]{1,0:T(8,128)(2,1)S(1)}, bf16[400,128]{1,0:T(8,128)(2,1)S(1)}, u32[]{:S(2)}, u32[]{:S(2)}) %collective-permute-start.29) | collective-permute-done | bytes 102432 | tf_op jit(solution)/shard_map/ppermute | solution.py:281
  140.2 2.6 %collective-permute-start.33 = (bf16[1600,128]{1,0:T(8,128)(2,1)S(1)}, bf16[1600,128]{1,0:T(8,128)(2,1)S(1)}, u32[]{:S(2)}, u32[]{:S(2)}) collective-permute-start(bf16[1600,128]{1,0:T(8,128)(2,1)S(1)} %shard_map.183.p0), channel_id=1, source_target_pairs={{0,6},{1,7},{2,0},{3,1},{4,2},{5,3},{6,4},{7,5},{8,14},{9,15},{10,... | collective-permute-start | bytes 1228808 | tf_op jit(solution)/shard_map/ppermute | solution.py:272
  143.4 5.3 %collective-permute-start.34 = (bf16[1600,128]{1,0:T(8,128)(2,1)S(1)}, bf16[1600,128]{1,0:T(8,128)(2,1)S(1)}, u32[]{:S(2)}, u32[]{:S(2)}) collective-permute-start(bf16[1600,128]{1,0:T(8,128)(2,1)S(1)} %shard_map.183.p0), channel_id=1, source_target_pairs={{0,1},{1,0},{2,3},{3,2},{4,5},{5,4},{6,7},{7,6},{8,9},{9,8},{10,11... | collective-permute-start | bytes 1228808 | tf_op jit(solution)/shard_map/ppermute | solution.py:276
  150.8 10.5 %collective-permute-start.37 = (bf16[1600,128]{1,0:T(8,128)(2,1)S(1)}, bf16[1600,128]{1,0:T(8,128)(2,1)S(1)}, u32[]{:S(2)}, u32[]{:S(2)}) collective-permute-start(bf16[1600,128]{1,0:T(8,128)(2,1)S(1)} %collective-permute-done.33.p3), channel_id=1, source_target_pairs={{0,1},{1,0},{2,3},{3,2},{4,5},{5,4},{6,7},{7,6},{8,9},{9,8},{10,11... | collective-permute-start | bytes 1228808 | tf_op jit(solution)/shard_map/ppermute | solution.py:276
  166.6 4.6 %shard_map.184 = (f32[2048,512]{1,0:T(8,128)}, f32[64,512]{1,0:T(8,128)}, f32[64,512]{1,0:T(8,128)}, f32[512,1024]{1,0:T(8,128)}) custom-call(s32[2]{0:T(128)S(1)} %pad_add_fusion.xc, bf16[1600,128]{1,0:T(8,128)(2,1)S(1)} %shard_map.183.p0, bf16[1600,128]{1,0:T(8,128)(2,1)S(1)} %collective-permute-done.31.p1, ...), custom_call_target="tpu_custom_call" | custom-call | bytes 9830408 | tf_op jit(solution)/shard_map/pallas_call | solution.py:29
  (151 shorter events, 68.0 us)
Async XLA Ops:
  7.2 51.6 %all-gather.3.cloned.1.call-start = ((), (), s32[]{:S(2)}) async-start(), calls=%async_computation.2 | async-start | bytes 1179648 | tf_op jit(solution)/shard_map/all_gather | solution.py:303
  7.9 156.7 %reduce-scatter.2.cloned.1.call-start = ((), (), s32[]{:S(2)}) async-start(), calls=%async_computation.1 | async-start | bytes 589824 | tf_op jit(solution)/shard_map/reduce_scatter | solution.py:377
  8.0 8.7 %collective-permute-start.2 = (bf16[64,1024]{1,0:T(8,128)(2,1)}, bf16[64,1024]{1,0:T(8,128)(2,1)}, u32[]{:S(2)}, u32[]{:S(2)}) collective-permute-start(bf16[64,1024]{1,0:T(8,128)(2,1)} %bitcast.22), channel_id=1, source_target_pairs={{0,6},{1,7},{2,0},{3,1},{4,2},{5,3},{6,4},{7,5},{8,14},{9,15},{10,... | collective-permute-start | bytes 393224 | tf_op jit(solution)/shard_map/ppermute | solution.py:272
  11.9 9.3 %collective-permute-start = (bf16[64,1024]{1,0:T(8,128)(2,1)}, bf16[64,1024]{1,0:T(8,128)(2,1)}, u32[]{:S(2)}, u32[]{:S(2)}) collective-permute-start(bf16[64,1024]{1,0:T(8,128)(2,1)} %bitcast.24), channel_id=1, source_target_pairs={{0,2},{1,3},{2,4},{3,5},{4,6},{5,7},{6,0},{7,1},{8,10},{9,11},{10,... | collective-permute-start | bytes 393224 | tf_op jit(solution)/shard_map/ppermute | solution.py:272
  12.5 26.1 %collective-permute-start.3 = (bf16[64,1024]{1,0:T(8,128)(2,1)}, bf16[64,1024]{1,0:T(8,128)(2,1)}, u32[]{:S(2)}, u32[]{:S(2)}) collective-permute-start(bf16[64,1024]{1,0:T(8,128)(2,1)} %bitcast.25), channel_id=1, source_target_pairs={{0,1},{1,0},{2,3},{3,2},{4,5},{5,4},{6,7},{7,6},{8,9},{9,8},{10,11... | collective-permute-start | bytes 393224 | tf_op jit(solution)/shard_map/ppermute | solution.py:276
  16.6 21.9 %collective-permute-start.6 = (bf16[64,1024]{1,0:T(8,128)(2,1)}, bf16[64,1024]{1,0:T(8,128)(2,1)}, u32[]{:S(2)}, u32[]{:S(2)}) collective-permute-start(bf16[64,1024]{1,0:T(8,128)(2,1)} %collective-permute-done.2.n3), channel_id=1, source_target_pairs={{0,1},{1,0},{2,3},{3,2},{4,5},{5,4},{6,7},{7,6},{8,9},{9,8},{10,11... | collective-permute-start | bytes 393224 | tf_op jit(solution)/shard_map/ppermute | solution.py:276
  18.2 20.4 %collective-permute-start.5 = (bf16[64,1024]{1,0:T(8,128)(2,1)}, bf16[64,1024]{1,0:T(8,128)(2,1)}, u32[]{:S(2)}, u32[]{:S(2)}) collective-permute-start(bf16[64,1024]{1,0:T(8,128)(2,1)} %collective-permute-done.1.n2), channel_id=1, source_target_pairs={{0,1},{1,0},{2,3},{3,2},{4,5},{5,4},{6,7},{7,6},{8,9},{9,8},{10,11... | collective-permute-start | bytes 393224 | tf_op jit(solution)/shard_map/ppermute | solution.py:276
  21.2 17.4 %collective-permute-start.4 = (bf16[64,1024]{1,0:T(8,128)(2,1)}, bf16[64,1024]{1,0:T(8,128)(2,1)}, u32[]{:S(2)}, u32[]{:S(2)}) collective-permute-start(bf16[64,1024]{1,0:T(8,128)(2,1)} %collective-permute-done.n1), channel_id=1, source_target_pairs={{0,1},{1,0},{2,3},{3,2},{4,5},{5,4},{6,7},{7,6},{8,9},{9,8},{10,11... | collective-permute-start | bytes 393224 | tf_op jit(solution)/shard_map/ppermute | solution.py:276
  47.6 9.6 %collective-permute-start.7 = (bf16[512,128]{1,0:T(8,128)(2,1)}, bf16[512,128]{1,0:T(8,128)(2,1)}, u32[]{:S(2)}, u32[]{:S(2)}) collective-permute-start(bf16[512,128]{1,0:T(8,128)(2,1)} %get-tuple-element.46.d0), channel_id=1, source_target_pairs={{0,2},{1,3},{2,4},{3,5},{4,6},{5,7},{6,0},{7,1},{8,10},{9,11},{10,... | collective-permute-start | bytes 393224 | tf_op jit(solution)/shard_map/ppermute | solution.py:272
  49.1 16.1 %collective-permute-start.10 = (bf16[512,128]{1,0:T(8,128)(2,1)}, bf16[512,128]{1,0:T(8,128)(2,1)}, u32[]{:S(2)}, u32[]{:S(2)}) collective-permute-start(bf16[512,128]{1,0:T(8,128)(2,1)} %get-tuple-element.46.d0), channel_id=1, source_target_pairs={{0,1},{1,0},{2,3},{3,2},{4,5},{5,4},{6,7},{7,6},{8,9},{9,8},{10,11... | collective-permute-start | bytes 393224 | tf_op jit(solution)/shard_map/ppermute | solution.py:276
  52.2 13.0 %collective-permute-start.13 = (bf16[512,128]{1,0:T(8,128)(2,1)}, bf16[512,128]{1,0:T(8,128)(2,1)}, u32[]{:S(2)}, u32[]{:S(2)}) collective-permute-start(bf16[512,128]{1,0:T(8,128)(2,1)} %collective-permute-done.9.d3), channel_id=1, source_target_pairs={{0,1},{1,0},{2,3},{3,2},{4,5},{5,4},{6,7},{7,6},{8,9},{9,8},{10,11... | collective-permute-start | bytes 393224 | tf_op jit(solution)/shard_map/ppermute | solution.py:276
  53.7 11.6 %collective-permute-start.12 = (bf16[512,128]{1,0:T(8,128)(2,1)}, bf16[512,128]{1,0:T(8,128)(2,1)}, u32[]{:S(2)}, u32[]{:S(2)}) collective-permute-start(bf16[512,128]{1,0:T(8,128)(2,1)} %collective-permute-done.8.d2), channel_id=1, source_target_pairs={{0,1},{1,0},{2,3},{3,2},{4,5},{5,4},{6,7},{7,6},{8,9},{9,8},{10,11... | collective-permute-start | bytes 393224 | tf_op jit(solution)/shard_map/ppermute | solution.py:276
  57.2 8.1 %collective-permute-start.11 = (bf16[512,128]{1,0:T(8,128)(2,1)}, bf16[512,128]{1,0:T(8,128)(2,1)}, u32[]{:S(2)}, u32[]{:S(2)}) collective-permute-start(bf16[512,128]{1,0:T(8,128)(2,1)} %collective-permute-done.7.d1), channel_id=1, source_target_pairs={{0,1},{1,0},{2,3},{3,2},{4,5},{5,4},{6,7},{7,6},{8,9},{9,8},{10,11... | collective-permute-start | bytes 393224 | tf_op jit(solution)/shard_map/ppermute | solution.py:276
  81.4 9.0 %collective-permute-start.15 = (bf16[512,128]{1,0:T(8,128)(2,1)S(1)}, bf16[512,128]{1,0:T(8,128)(2,1)S(1)}, u32[]{:S(2)}, u32[]{:S(2)}) collective-permute-start(bf16[512,128]{1,0:T(8,128)(2,1)S(1)} %get-tuple-element.62), channel_id=1, source_target_pairs={{0,2},{1,3},{2,4},{3,5},{4,6},{5,7},{6,0},{7,1},{8,10},{9,11},{10,... | collective-permute-start | bytes 393224 | tf_op jit(solution)/shard_map/ppermute | solution.py:272
  81.4 9.0 %collective-permute-start.16 = (bf16[512,128]{1,0:T(8,128)(2,1)S(1)}, bf16[512,128]{1,0:T(8,128)(2,1)S(1)}, u32[]{:S(2)}, u32[]{:S(2)}) collective-permute-start(bf16[512,128]{1,0:T(8,128)(2,1)S(1)} %get-tuple-element.63), channel_id=1, source_target_pairs={{0,4},{1,5},{2,6},{3,7},{4,0},{5,1},{6,2},{7,3},{8,12},{9,13},{10,... | collective-permute-start | bytes 393224 | tf_op jit(solution)/shard_map/ppermute | solution.py:272
  83.4 7.4 %collective-permute-start.17 = (bf16[512,128]{1,0:T(8,128)(2,1)S(1)}, bf16[512,128]{1,0:T(8,128)(2,1)S(1)}, u32[]{:S(2)}, u32[]{:S(2)}) collective-permute-start(bf16[512,128]{1,0:T(8,128)(2,1)S(1)} %get-tuple-element.64), channel_id=1, source_target_pairs={{0,6},{1,7},{2,0},{3,1},{4,2},{5,3},{6,4},{7,5},{8,14},{9,15},{10,... | collective-permute-start | bytes 393224 | tf_op jit(solution)/shard_map/ppermute | solution.py:272
  98.0 8.0 %collective-permute-start.19 = (bf16[832,128]{1,0:T(8,128)(2,1)}, bf16[832,128]{1,0:T(8,128)(2,1)}, u32[]{:S(2)}, u32[]{:S(2)}) collective-permute-start(bf16[832,128]{1,0:T(8,128)(2,1)} %get-tuple-element.72), channel_id=1, source_target_pairs={{0,2},{1,3},{2,4},{3,5},{4,6},{5,7},{6,0},{7,1},{8,10},{9,11},{10,... | collective-permute-start | bytes 638984 | tf_op jit(solution)/shard_map/ppermute | solution.py:272
  98.0 13.1 %collective-permute-start.20 = (bf16[832,128]{1,0:T(8,128)(2,1)}, bf16[832,128]{1,0:T(8,128)(2,1)}, u32[]{:S(2)}, u32[]{:S(2)}) collective-permute-start(bf16[832,128]{1,0:T(8,128)(2,1)} %get-tuple-element.73), channel_id=1, source_target_pairs={{0,4},{1,5},{2,6},{3,7},{4,0},{5,1},{6,2},{7,3},{8,12},{9,13},{10,... | collective-permute-start | bytes 638984 | tf_op jit(solution)/shard_map/ppermute | solution.py:272
  101.3 9.9 %collective-permute-start.21 = (bf16[832,128]{1,0:T(8,128)(2,1)}, bf16[832,128]{1,0:T(8,128)(2,1)}, u32[]{:S(2)}, u32[]{:S(2)}) collective-permute-start(bf16[832,128]{1,0:T(8,128)(2,1)} %get-tuple-element.74), channel_id=1, source_target_pairs={{0,6},{1,7},{2,0},{3,1},{4,2},{5,3},{6,4},{7,5},{8,14},{9,15},{10,... | collective-permute-start | bytes 638984 | tf_op jit(solution)/shard_map/ppermute | solution.py:272
  140.2 10.6 %collective-permute-start.33 = (bf16[1600,128]{1,0:T(8,128)(2,1)S(1)}, bf16[1600,128]{1,0:T(8,128)(2,1)S(1)}, u32[]{:S(2)}, u32[]{:S(2)}) collective-permute-start(bf16[1600,128]{1,0:T(8,128)(2,1)S(1)} %shard_map.183.p0), channel_id=1, source_target_pairs={{0,6},{1,7},{2,0},{3,1},{4,2},{5,3},{6,4},{7,5},{8,14},{9,15},{10,... | collective-permute-start | bytes 1228808 | tf_op jit(solution)/shard_map/ppermute | solution.py:272
  142.8 18.5 %collective-permute-start.32 = (bf16[1600,128]{1,0:T(8,128)(2,1)S(1)}, bf16[1600,128]{1,0:T(8,128)(2,1)S(1)}, u32[]{:S(2)}, u32[]{:S(2)}) collective-permute-start(bf16[1600,128]{1,0:T(8,128)(2,1)S(1)} %shard_map.183.p0), channel_id=1, source_target_pairs={{0,4},{1,5},{2,6},{3,7},{4,0},{5,1},{6,2},{7,3},{8,12},{9,13},{10,... | collective-permute-start | bytes 1228808 | tf_op jit(solution)/shard_map/ppermute | solution.py:272
  142.8 20.3 %collective-permute-start.31 = (bf16[1600,128]{1,0:T(8,128)(2,1)S(1)}, bf16[1600,128]{1,0:T(8,128)(2,1)S(1)}, u32[]{:S(2)}, u32[]{:S(2)}) collective-permute-start(bf16[1600,128]{1,0:T(8,128)(2,1)S(1)} %shard_map.183.p0), channel_id=1, source_target_pairs={{0,2},{1,3},{2,4},{3,5},{4,6},{5,7},{6,0},{7,1},{8,10},{9,11},{10,... | collective-permute-start | bytes 1228808 | tf_op jit(solution)/shard_map/ppermute | solution.py:272
  143.4 23.1 %collective-permute-start.34 = (bf16[1600,128]{1,0:T(8,128)(2,1)S(1)}, bf16[1600,128]{1,0:T(8,128)(2,1)S(1)}, u32[]{:S(2)}, u32[]{:S(2)}) collective-permute-start(bf16[1600,128]{1,0:T(8,128)(2,1)S(1)} %shard_map.183.p0), channel_id=1, source_target_pairs={{0,1},{1,0},{2,3},{3,2},{4,5},{5,4},{6,7},{7,6},{8,9},{9,8},{10,11... | collective-permute-start | bytes 1228808 | tf_op jit(solution)/shard_map/ppermute | solution.py:276
  150.8 15.8 %collective-permute-start.37 = (bf16[1600,128]{1,0:T(8,128)(2,1)S(1)}, bf16[1600,128]{1,0:T(8,128)(2,1)S(1)}, u32[]{:S(2)}, u32[]{:S(2)}) collective-permute-start(bf16[1600,128]{1,0:T(8,128)(2,1)S(1)} %collective-permute-done.33.p3), channel_id=1, source_target_pairs={{0,1},{1,0},{2,3},{3,2},{4,5},{5,4},{6,7},{7,6},{8,9},{9,8},{10,11... | collective-permute-start | bytes 1228808 | tf_op jit(solution)/shard_map/ppermute | solution.py:276
  (49 other events, 331.7 us)
Sparse Core Ops, SparseCore 0:
  9.7 26.9 all-gather.2
  101.4 30.3 reduce-scatter.1
